TPU v7x, 256 devices: a whole 4x4x8 slice. The times are simulated.
256 devices in a mesh: row: 8 (over y, core), col: 32 (over x, z).
Axes of the slice: x: 4, y: 4, z: 8, core: 2. Of those that a mesh axis runs over, the one named last changes fastest.
Arguments:
- quant_acts: bfloat16 [4096, 8192], P('col', 'row'), may hold values from -6 to 6
- full_acts: bfloat16 [4096, 8192], P('col', 'row'), may hold values from -6 to 6
Outputs:
- hessian: float32 [8192, 8192], P('row', 'col')
- cross_term: float32 [8192, 8192], P('row', 'col')
All inputs are finite; a program needn't handle non-finite values.
Results may differ from a plain program's by a relative error of at most 0.0028.
Values may be sent and summed in bfloat16 or wider, within the bound.
A program may use at most 64 MiB of HBM per device.

v0:
```python
import jax
import jax.numpy as jnp
from jax import lax
from jax.sharding import PartitionSpec as P


def transposed(left_side, right_side):
    return lax.dot_general(
        left_side, right_side, (((0,), (0,)), ((), ())), preferred_element_type=jnp.float32
    )


def local(quant_acts, full_acts):
    deltas = (full_acts.astype(jnp.float32) - quant_acts.astype(jnp.float32)).astype(jnp.bfloat16)
    slab_wide = lax.all_gather(quant_acts, "row", axis=1, tiled=True)
    column_ops = lax.all_to_all(slab_wide, "col", split_axis=1, concat_axis=0, tiled=True)
    total_tokens = column_ops.shape[0]
    hessian = transposed(lax.all_gather(quant_acts, "col", axis=0, tiled=True), column_ops)
    cross_term = transposed(lax.all_gather(deltas, "col", axis=0, tiled=True), column_ops)
    scale = 1.0 / total_tokens
    return (hessian * scale, cross_term * scale)


def solution(mesh):
    return jax.shard_map(
        local,
        mesh=mesh,
        in_specs=(P("col", "row"), P("col", "row")),
        out_specs=(P("row", "col"), P("row", "col")),
        check_vma=False,
    )
```

profile of v0, /device:TPU:2, one launch (start us, length us, event | category | flops | bytes accessed | tf_op | source)
XLA Modules:
  0.0 268.5 jit_solution(14642137038211381502)
XLA Ops:
  7.2 0.0 all-gather.6.cloned.1.call-start
  7.2 1.8 copy.4
  9.0 0.0 all-gather.6.cloned.1.call-update
  9.0 0.0 all-gather.8.cloned.1.call-start
  9.1 1.8 subtract_convert_fusion
  10.9 0.0 all-gather.8.cloned.1.call-update
  10.9 0.0 all-gather.4.cloned.1.call-start
  11.0 0.7 all-gather.4.cloned.1.call-update
  11.6 29.5 %all-gather.6.cloned.1.call-done = bf16[128,8192]{0,1:T(8,128)(2,1)} async-done(((bf16[128,1024]{0,1:T(8,128)(2,1)}), bf16[128,8192]{0,1:T(8,128)(2,1)}) %all-gather.6.cloned.1.call-update) | async-done | bytes 2097168 | tf_op jit(solution)/shard_map/all_gather | solution.py:15
  41.2 69.0 %all_to_all.19 = bf16[128,32,256]{0,2,1:T(8,128)(2,1)} all-to-all(bf16[128,32,256]{0,2,1:T(8,128)(2,1)} %bitcast.10), channel_id=1, replica_groups=mesh['row'=8,'col'=32] {'col'}, dimensions={1} | all-to-all | bytes 4194304 | tf_op jit(solution)/shard_map/all_to_all | solution.py:16
  110.2 3.5 %copy.5 = bf16[32,128,256]{2,1,0:T(8,128)(2,1)S(1)} copy(bf16[32,128,256]{1,2,0:T(8,128)(2,1)} %bitcast.9) | data formatting | bytes 4194304 | tf_op jit(solution)/shard_map/all_to_all | solution.py:16
  113.7 43.5 %all-gather.8.cloned.1.call-done = bf16[4096,1024]{1,0:T(8,128)(2,1)} async-done(((bf16[128,1024]{1,0:T(8,128)(2,1)}), bf16[4096,1024]{1,0:T(8,128)(2,1)}) %all-gather.8.cloned.1.call-update) | async-done | bytes 8388624 | tf_op jit(solution)/shard_map/all_gather | solution.py:19
  157.2 6.7 %convolution_multiply_fusion = f32[1024,256]{1,0:T(8,128)} fusion(bf16[4096,1024]{1,0:T(8,128)(2,1)} %all-gather.8.cloned.1.call-done, bf16[4096,256]{1,0:T(8,128)(2,1)S(1)} %bitcast.7), kind=kOutput, calls=%fused_computation | convolution fusion | flops 2147745792 | bytes 11534336 | tf_op jit(solution)/shard_map/dot_general | solution.py:8
  163.9 91.3 %all-gather.4.cloned.1.call-done = bf16[4096,1024]{1,0:T(8,128)(2,1)} async-done(((bf16[128,1024]{1,0:T(8,128)(2,1)}), bf16[4096,1024]{1,0:T(8,128)(2,1)}) %all-gather.4.cloned.1.call-update) | async-done | bytes 8388624 | tf_op jit(solution)/shard_map/all_gather | solution.py:18
  255.2 6.7 %convolution_multiply_fusion.1 = f32[1024,256]{1,0:T(8,128)} fusion(bf16[4096,1024]{1,0:T(8,128)(2,1)} %all-gather.4.cloned.1.call-done, bf16[4096,256]{1,0:T(8,128)(2,1)S(1)} %bitcast.8), kind=kOutput, calls=%fused_computation.1 | convolution fusion | flops 2147745792 | bytes 11534336 | tf_op jit(solution)/shard_map/dot_general | solution.py:8
Async XLA Ops:
  7.2 34.0 %all-gather.6.cloned.1.call-start = ((), (), s32[]{:S(2)}) async-start(), calls=%async_computation.2 | async-start | bytes 2359296 | tf_op jit(solution)/shard_map/all_gather | solution.py:15
  9.0 148.2 %all-gather.8.cloned.1.call-start = ((), (), s32[]{:S(2)}) async-start(), calls=%async_computation.3 | async-start | bytes 8650752 | tf_op jit(solution)/shard_map/all_gather | solution.py:19
  10.9 244.3 %all-gather.4.cloned.1.call-start = ((), (), s32[]{:S(2)}) async-start(), calls=%async_computation.1 | async-start | bytes 8650752 | tf_op jit(solution)/shard_map/all_gather | solution.py:18
Sparse Core Ops, SparseCore 0:
  10.4 30.6 all-gather.5
  44.3 112.8 all-gather.7
  159.8 95.3 all-gather.3
where the time goes:
time: 270 us; the launch traced here: 268 us
  waiting for transfers between devices  165 us (61%)
  blocking collectives  69 us (26%)
  between operations  13.8 us (5%)
  matrix products  13.4 us (5%)
  local copies, waits for them, and re-layouts  5.27 us (2%)
    all_gather x1, waiting for transfers between devices, local(): lax.all_gather(quant_acts, 'col', axis=0, tiled=True)  91.3 us
    all_to_all x1, blocking collectives, local(): lax.all_to_all(slab_wide, 'col', split_axis=1, concat_axis=0, tiled=True)  69 us
    all_gather x1, waiting for transfers between devices, local(): lax.all_gather(deltas, 'col', axis=0, tiled=True)  43.5 us
    all_gather x1, waiting for transfers between devices, local(): slab_wide = lax.all_gather(quant_acts, 'row', axis=1, tiled=True)  29.5 us
    dot_general x2, matrix products, transposed(): lax.dot_general(left_side, right_side, (((0,), (0,)), ((), ())), preferre...  13.4 us
  transfers between devices with their start and end apart: 3, of which 3 were waited for; matrix products, arithmetic and copies ran while one was open for 4% of the time, Pallas kernels for 0%

commit v1 on v0

v1 whole, which is shorter than its diff:
```python
import jax
import jax.numpy as jnp
from jax import lax
from jax.experimental import pallas as pl
from jax.experimental.pallas import tpu as pltpu
from jax.sharding import PartitionSpec as P

MESH = pl.DeviceIdType.MESH
NX, NY, NZ = 4, 4, 8
TOK, FEAT, SUB = 128, 1024, 256
CH = 128
NQ = FEAT // CH
NJ = 2 * NQ
HALF = CH // 2
ORDER = (1, 7, 2, 6, 3, 5, 4)


def wrap(v, n):
    return lax.rem(v + n, n)


def kernel(q_ref, f_ref, o_ref, rows, cols, part, s1, r1, s2, r2,
           zsend, zrecv, asend, arecv, ysend, yrecv, ksend, krecv, xsend, xrecv):
    r, c = lax.axis_index("row"), lax.axis_index("col")
    y, k = lax.div(r, 2), lax.rem(r, 2)
    x, z = lax.div(c, NZ), lax.rem(c, NZ)
    xr, xl, xo = wrap(x + 1, NX), wrap(x - 1, NX), wrap(x + 2, NX)
    yr, yl, yo = wrap(y + 1, NY), wrap(y - 1, NY), wrap(y + 2, NY)
    zr, zl = wrap(z + 1, NZ), wrap(z - 1, NZ)
    owner = lax.div(z, 4) == k

    def dev(x, y, z, k):
        return (y * 2 + k, x * NZ + z)

    right, left = dev(x, y, zr, k), dev(x, y, zl, k)
    xright, xleft = dev(xr, y, z, k), dev(xl, y, z, k)
    up, down = dev(x, yr, z, k), dev(x, yl, z, k)
    other = dev(x, y, z, 1 - k)

    def remote(src, dst, send, recv, to):
        return pltpu.make_async_remote_copy(
            src_ref=src, dst_ref=dst, send_sem=send, recv_sem=recv, device_id=to, device_id_type=MESH
        )

    barrier = pltpu.get_barrier_semaphore()
    for d in range(1, NZ):
        pl.semaphore_signal(barrier, inc=1, device_id=dev(x, y, wrap(z + d, NZ), k), device_id_type=MESH)
    for to in (xright, xleft, up, down, other):
        pl.semaphore_signal(barrier, inc=1, device_id=to, device_id_type=MESH)

    for j in range(NQ):
        qj = q_ref[:, j * CH : (j + 1) * CH].astype(jnp.float32)
        fj = f_ref[:, j * CH : (j + 1) * CH].astype(jnp.float32)
        rows[j, z] = qj.T.astype(jnp.bfloat16)
        rows[NQ + j, z] = (fj - qj).astype(jnp.bfloat16).astype(jnp.float32).T.astype(jnp.bfloat16)

    pl.semaphore_wait(barrier, NZ - 1 + 5)

    def zcopy(j, s, way):
        at = wrap(z - s, NZ) if way == 0 else lax.rem(z + s, NZ)
        ref = rows.at[j, at]
        if s == 3:
            ref = rows.at[j, at, pl.ds(way * HALF, HALF)]
        return remote(ref, ref, zsend.at[j, s, way], zrecv.at[j, s, way], (right, left)[way])

    def zarrived(j, s, way):
        at = wrap(z - s - 1, NZ) if way == 0 else lax.rem(z + s + 1, NZ)
        ref = rows.at[j, at]
        if s == 3:
            ref = rows.at[j, at, pl.ds(way * HALF, HALF)]
        remote(ref, ref, zsend.at[j, s, way], zrecv.at[j, s, way], (right, left)[way]).wait_recv()

    def zslot(t, guard=True):
        for s in range(4):
            j = t - s

            def go(j=j, s=s):
                for way in range(2):
                    if s > 0:
                        zarrived(j, s - 1, way)
                    zcopy(j, s, way).start()

            if guard:
                pl.when(jnp.logical_and(j >= 0, j < NJ))(go)
            elif j >= 0:
                go()

    def acopy(d):
        to = wrap(z + d, NZ)
        src = q_ref.at[:, pl.ds(pl.multiple_of(lax.rem(to, 4) * SUB, SUB), SUB)]
        return remote(src, cols.at[y, z], asend.at[d - 1], arecv.at[d - 1], dev(x, y, to, k))

    for d in ORDER:
        pl.when(lax.div(wrap(z + d, NZ), 4) == k)(lambda d=d: acopy(d).start())

    zslot(0, False)

    @pl.when(owner)
    def _():
        cols[y, z] = q_ref[:, pl.ds(pl.multiple_of(lax.rem(z, 4) * SUB, SUB), SUB)]

    zslot(1, False)

    def ycopy(b, i, s, way):
        if s == 0:
            ref = cols.at[y, b]
        else:
            ref = cols.at[(yl, yr)[way], b, pl.ds(way * 64, 64)]
        return remote(ref, ref, ysend.at[i, s, way], yrecv.at[i, s, way], (up, down)[way])

    def yarrived(b, i, s, way):
        if s == 0:
            ref = cols.at[(yl, yr)[way], b]
        else:
            ref = cols.at[yo, b, pl.ds(way * 64, 64)]
        remote(ref, ref, ysend.at[i, s, way], yrecv.at[i, s, way], (up, down)[way]).wait_recv()

    def kcopy(yb, b, i, n):
        ref = cols.at[yb, b]
        return remote(ref, ref, ksend.at[i, n], krecv.at[i, n], other)

    SRC = (0,) + ORDER

    @pl.when(owner)
    def _():
        for i, d in enumerate(SRC):
            b = wrap(z - d, NZ)
            if d:
                remote(cols.at[y, b], cols.at[y, b], asend.at[d - 1], arecv.at[d - 1], other).wait_recv()
            ycopy(b, i, 0, 0).start()
            ycopy(b, i, 0, 1).start()
            kcopy(y, b, i, 0).start()

    zslot(2, False)

    @pl.when(owner)
    def _():
        for i, d in enumerate(SRC):
            b = wrap(z - d, NZ)
            for way in range(2):
                yarrived(b, i, 0, way)
                ycopy(b, i, 1, way).start()
                kcopy((yl, yr)[way], b, i, 1 + way).start()

    zslot(3, False)

    @pl.when(owner)
    def _():
        for i, d in enumerate(SRC):
            b = wrap(z - d, NZ)
            for way in range(2):
                yarrived(b, i, 1, way)
            kcopy(yo, b, i, 3).start()

    @pl.when(jnp.logical_not(owner))
    def _():
        for i, d in enumerate(SRC):
            b = wrap(z - d, NZ)
            for n, yb in enumerate((y, yl, yr, yo)):
                kcopy(yb, b, i, n).wait_recv()

    def x1copy(j, way):
        return remote(s1.at[j, way], r1.at[j, way], xsend.at[j, 0, way], xrecv.at[j, 0, way], (xright, xleft)[way])

    def x2copy(j, way):
        return remote(s2.at[j, way], r2.at[j, way], xsend.at[j, 1, way], xrecv.at[j, 1, way], (xright, xleft)[way])

    def product(j):
        for way in range(2):
            zarrived(j, 3, way)
        a = jnp.concatenate([rows[j, b] for b in range(NZ)], axis=1)

        def times(dest):
            b = cols[dest].reshape(NZ * TOK, SUB)
            return jnp.dot(a, b, preferred_element_type=jnp.float32)

        far = times(xo).astype(jnp.bfloat16)
        s1[j, 0] = far[:HALF]
        s1[j, 1] = far[HALF:]
        x1copy(j, 0).start()
        x1copy(j, 1).start()
        slot = lax.rem(j, 4)
        part[slot, 0] = times(xr)
        part[slot, 1] = times(xl)
        part[slot, 2] = times(x)

    def pass_on(j):
        slot = lax.rem(j, 4)
        x1copy(j, 0).wait_recv()
        s2[j, 0, :HALF] = (part[slot, 0, :HALF] + r1[j, 0].astype(jnp.float32)).astype(jnp.bfloat16)
        s2[j, 0, HALF:] = part[slot, 0, HALF:].astype(jnp.bfloat16)
        x2copy(j, 0).start()
        x1copy(j, 1).wait_recv()
        s2[j, 1, HALF:] = (part[slot, 1, HALF:] + r1[j, 1].astype(jnp.float32)).astype(jnp.bfloat16)
        s2[j, 1, :HALF] = part[slot, 1, :HALF].astype(jnp.bfloat16)
        x2copy(j, 1).start()

    def finish(j):
        slot = lax.rem(j, 4)
        x2copy(j, 0).wait_recv()
        x2copy(j, 1).wait_recv()
        total = part[slot, 2] + r2[j, 0].astype(jnp.float32) + r2[j, 1].astype(jnp.float32)
        o_ref[pl.ds(pl.multiple_of(j * CH, CH), CH), :] = total

    def slot(t, carry):
        zslot(t)
        for lag, work in ((4, product), (5, pass_on), (6, finish)):
            j = t - lag
            pl.when(jnp.logical_and(j >= 0, j < NJ))(lambda j=j, work=work: work(j))
        return carry

    lax.fori_loop(4, NJ + 6, slot, 0)

    def drain(j, carry):
        for way in range(2):
            for s in range(4):
                zcopy(j, s, way).wait_send()
            x1copy(j, way).wait_send()
            x2copy(j, way).wait_send()
        return carry

    lax.fori_loop(0, NJ, drain, 0)
    for d in ORDER:
        pl.when(lax.div(wrap(z + d, NZ), 4) == k)(lambda d=d: acopy(d).wait_send())

    @pl.when(owner)
    def _():
        for i, d in enumerate(SRC):
            b = wrap(z - d, NZ)
            for way in range(2):
                ycopy(b, i, 0, way).wait_send()
                ycopy(b, i, 1, way).wait_send()
            for n, yb in enumerate((y, yl, yr, yo)):
                kcopy(yb, b, i, n).wait_send()


def local(quant_acts, full_acts):
    bf16, f32, dma = jnp.bfloat16, jnp.float32, pltpu.SemaphoreType.DMA
    out = pl.pallas_call(
        kernel,
        out_shape=jax.ShapeDtypeStruct((2 * FEAT, SUB), f32),
        in_specs=[pl.BlockSpec(memory_space=pltpu.VMEM)] * 2,
        out_specs=pl.BlockSpec(memory_space=pltpu.VMEM),
        scratch_shapes=[
            pltpu.VMEM((NJ, NZ, CH, TOK), bf16),
            pltpu.VMEM((NY, NZ, TOK, SUB), bf16),
            pltpu.VMEM((4, 3, CH, SUB), f32),
            pltpu.VMEM((NJ, 2, HALF, SUB), bf16),
            pltpu.VMEM((NJ, 2, HALF, SUB), bf16),
            pltpu.VMEM((NJ, 2, CH, SUB), bf16),
            pltpu.VMEM((NJ, 2, CH, SUB), bf16),
            dma((NJ, 4, 2)),
            dma((NJ, 4, 2)),
            dma((NZ - 1,)),
            dma((NZ - 1,)),
            dma((NZ, 2, 2)),
            dma((NZ, 2, 2)),
            dma((NZ, 4)),
            dma((NZ, 4)),
            dma((NJ, 2, 2)),
            dma((NJ, 2, 2)),
        ],
        compiler_params=pltpu.CompilerParams(
            collective_id=0, has_side_effects=True, vmem_limit_bytes=48 * 2**20
        ),
        cost_estimate=pl.CostEstimate(
            flops=2 * 2 * FEAT * 1024 * 1024, bytes_accessed=3 * 2**20, transcendentals=0
        ),
        name="stats",
    )(quant_acts, full_acts)
    scale = 1.0 / (TOK * NX * NZ)
    return out[:FEAT] * scale, out[FEAT:] * scale


def solution(mesh):
    return jax.shard_map(
        local,
        mesh=mesh,
        in_specs=(P("col", "row"), P("col", "row")),
        out_specs=(P("row", "col"), P("row", "col")),
        check_vma=False,
    )
```

time: 270 us -> 97 us (0.36)
  waiting for transfers between devices: 165 us -> 0 us
  Pallas kernels: 0 us -> 92.8 us
  blocking collectives: 69 us -> 0 us
  matrix products: 13.4 us -> 0 us
  between operations: 13.8 us -> 0.65 us
  local copies, waits for them, and re-layouts: 5.27 us -> 1.89 us
    all_gather x3 -> x0, waiting for transfers between devices: 164 us -> none  [the longest x1 91.3 us: local(): lax.all_gather(quant_acts, 'col', axis=0, tiled=True)]
    pallas_call x0 -> x1, Pallas kernels: none -> 92.8 us  [local(): pl.pallas_call(kernel, out_shape=jax.ShapeDtypeStruct((2 * FEAT, SUB), f3...]
    all_to_all x1 -> x0, blocking collectives: 69 us -> none  [local(): lax.all_to_all(slab_wide, 'col', split_axis=1, concat_axis=0, tiled=True)]
    dot_general x2 -> x0, matrix products: 13.4 us -> none  [transposed(): lax.dot_general(left_side, right_side, (((0,), (0,)), ((), ())), preferre...]
    all_to_all x1 -> x0, local copies, waits for them, and re-layouts: 3.48 us -> none  [local(): lax.all_to_all(slab_wide, 'col', split_axis=1, concat_axis=0, tiled=True)]
  transfers between devices with their start and end apart: 3 -> 0, of which waited for: 3 -> 0; matrix products, arithmetic and copies ran while one was open for 4% -> 0% of each run, Pallas kernels for 0% -> 0%
where the time goes in v1:
time: 97 us; the launch traced here: 96.8 us
  Pallas kernels  92.8 us (96%)
  local copies, waits for them, and re-layouts  1.89 us (2%)
  other arithmetic  1.45 us (1%)
    pallas_call x1, Pallas kernels, local(): pl.pallas_call(kernel, out_shape=jax.ShapeDtypeStruct((2 * FEAT, SUB), f3...  92.8 us

profile of v1, /device:TPU:2, one launch (start us, length us, event | category | flops | bytes accessed | tf_op | source)
XLA Modules:
  0.0 96.8 jit_solution(1663428118690251086)
XLA Ops:
  0.6 0.0 copy-start
  0.6 0.9 copy-done
  1.6 0.0 copy-start.1
  1.6 0.9 copy-done.1
  2.5 92.8 %stats.1 = f32[2048,256]{1,0:T(8,128)S(1)} custom-call(bf16[128,1024]{1,0:T(8,128)(2,1)S(1)} %copy-done, bf16[128,1024]{1,0:T(8,128)(2,1)S(1)} %copy-done.1), custom_call_target="tpu_custom_call" | custom-call | flops 4294967296 | bytes 3145728 | tf_op jit(solution)/shard_map/stats/pallas_call | solution.py:239
  95.4 1.5 %slice_multiply_fusion = (f32[1024,256]{1,0:T(8,128)}, f32[1024,256]{1,0:T(8,128)}) fusion(f32[2048,256]{1,0:T(8,128)S(1)} %stats.1), kind=kLoop, calls=%fused_computation | loop fusion | flops 524288 | bytes 4194304 | tf_op jit(solution)/shard_map/mul | solution.py:272
Async XLA Ops:
  0.6 1.0 copy-start
  1.6 0.9 copy-start.1

commit v2 on v1

--- a/solution.py
+++ b/solution.py
@@ -12,6 +12,12 @@
 NQ = FEAT // CH
 NJ = 2 * NQ
 HALF = CH // 2
+PIECES = 1
+ROWS = CH // PIECES
+LAG = 2
+XLAG = 2
+YLAG = 3
+PRE = 0
 ORDER = (1, 7, 2, 6, 3, 5, 4)
 
 
@@ -19,7 +25,7 @@
     return lax.rem(v + n, n)
 
 
-def kernel(q_ref, f_ref, o_ref, rows, cols, part, s1, r1, s2, r2,
+def kernel(q_hbm, f_hbm, o_ref, q_ref, f_ref, load, rows, cols, part, s1, r1, s2, r2,
            zsend, zrecv, asend, arecv, ysend, yrecv, ksend, krecv, xsend, xrecv):
     r, c = lax.axis_index("row"), lax.axis_index("col")
     y, k = lax.div(r, 2), lax.rem(r, 2)
@@ -42,12 +48,18 @@
             src_ref=src, dst_ref=dst, send_sem=send, recv_sem=recv, device_id=to, device_id_type=MESH
         )
 
+    loads = [pltpu.make_async_copy(a, b, load.at[i]) for i, (a, b) in enumerate(((q_hbm, q_ref), (f_hbm, f_ref)))]
+    for copy in loads:
+        copy.start()
+
     barrier = pltpu.get_barrier_semaphore()
     for d in range(1, NZ):
         pl.semaphore_signal(barrier, inc=1, device_id=dev(x, y, wrap(z + d, NZ), k), device_id_type=MESH)
     for to in (xright, xleft, up, down, other):
         pl.semaphore_signal(barrier, inc=1, device_id=to, device_id_type=MESH)
 
+    for copy in loads:
+        copy.wait()
     for j in range(NQ):
         qj = q_ref[:, j * CH : (j + 1) * CH].astype(jnp.float32)
         fj = f_ref[:, j * CH : (j + 1) * CH].astype(jnp.float32)
@@ -56,33 +68,33 @@
 
     pl.semaphore_wait(barrier, NZ - 1 + 5)
 
-    def zcopy(j, s, way):
-        at = wrap(z - s, NZ) if way == 0 else lax.rem(z + s, NZ)
-        ref = rows.at[j, at]
+    def zref(p, at, s, way):
+        j, start = lax.div(p, PIECES), lax.rem(p, PIECES) * ROWS
         if s == 3:
-            ref = rows.at[j, at, pl.ds(way * HALF, HALF)]
-        return remote(ref, ref, zsend.at[j, s, way], zrecv.at[j, s, way], (right, left)[way])
-
-    def zarrived(j, s, way):
-        at = wrap(z - s - 1, NZ) if way == 0 else lax.rem(z + s + 1, NZ)
-        ref = rows.at[j, at]
-        if s == 3:
-            ref = rows.at[j, at, pl.ds(way * HALF, HALF)]
-        remote(ref, ref, zsend.at[j, s, way], zrecv.at[j, s, way], (right, left)[way]).wait_recv()
+            return rows.at[j, at, pl.ds(pl.multiple_of(start + way * (ROWS // 2), ROWS // 2), ROWS // 2)]
+        return rows.at[j, at, pl.ds(pl.multiple_of(start, ROWS), ROWS)]
+
+    def zcopy(p, s, way):
+        ref = zref(p, wrap(z - s, NZ) if way == 0 else lax.rem(z + s, NZ), s, way)
+        return remote(ref, ref, zsend.at[p, s, way], zrecv.at[p, s, way], (right, left)[way])
+
+    def zarrived(p, s, way):
+        ref = zref(p, wrap(z - s - 1, NZ) if way == 0 else lax.rem(z + s + 1, NZ), s, way)
+        remote(ref, ref, zsend.at[p, s, way], zrecv.at[p, s, way], (right, left)[way]).wait_recv()
 
     def zslot(t, guard=True):
         for s in range(4):
-            j = t - s
-
-            def go(j=j, s=s):
+            p = t - s * LAG
+
+            def go(p=p, s=s):
                 for way in range(2):
                     if s > 0:
-                        zarrived(j, s - 1, way)
-                    zcopy(j, s, way).start()
+                        zarrived(p, s - 1, way)
+                    zcopy(p, s, way).start()
 
             if guard:
-                pl.when(jnp.logical_and(j >= 0, j < NJ))(go)
-            elif j >= 0:
+                pl.when(jnp.logical_and(p >= 0, p < NJ * PIECES))(go)
+            elif p >= 0:
                 go()
 
     def acopy(d):
@@ -93,13 +105,12 @@
     for d in ORDER:
         pl.when(lax.div(wrap(z + d, NZ), 4) == k)(lambda d=d: acopy(d).start())
 
-    zslot(0, False)
-
     @pl.when(owner)
     def _():
         cols[y, z] = q_ref[:, pl.ds(pl.multiple_of(lax.rem(z, 4) * SUB, SUB), SUB)]
 
-    zslot(1, False)
+    for t in range(PRE):
+        zslot(t, False)
 
     def ycopy(b, i, s, way):
         if s == 0:
@@ -121,36 +132,38 @@
 
     SRC = (0,) + ORDER
 
-    @pl.when(owner)
-    def _():
-        for i, d in enumerate(SRC):
+    def item(i):
+        if i < NZ:
+            d = SRC[i]
             b = wrap(z - d, NZ)
             if d:
                 remote(cols.at[y, b], cols.at[y, b], asend.at[d - 1], arecv.at[d - 1], other).wait_recv()
             ycopy(b, i, 0, 0).start()
             ycopy(b, i, 0, 1).start()
             kcopy(y, b, i, 0).start()
-
-    zslot(2, False)
-
-    @pl.when(owner)
-    def _():
-        for i, d in enumerate(SRC):
-            b = wrap(z - d, NZ)
+        if 0 <= i - YLAG < NZ:
+            n = i - YLAG
+            b = wrap(z - SRC[n], NZ)
             for way in range(2):
-                yarrived(b, i, 0, way)
-                ycopy(b, i, 1, way).start()
-                kcopy((yl, yr)[way], b, i, 1 + way).start()
-
-    zslot(3, False)
-
-    @pl.when(owner)
-    def _():
-        for i, d in enumerate(SRC):
-            b = wrap(z - d, NZ)
+                yarrived(b, n, 0, way)
+                ycopy(b, n, 1, way).start()
+                kcopy((yl, yr)[way], b, n, 1 + way).start()
+        if 0 <= i - 2 * YLAG < NZ:
+            n = i - 2 * YLAG
+            b = wrap(z - SRC[n], NZ)
             for way in range(2):
-                yarrived(b, i, 1, way)
-            kcopy(yo, b, i, 3).start()
+                yarrived(b, n, 1, way)
+            kcopy(yo, b, n, 3).start()
+
+    FIRST = 4 * LAG // PIECES
+    count, rest = NZ + 2 * YLAG, FIRST * PIECES - PRE
+    for n in range(rest):
+        @pl.when(owner)
+        def _():
+            for i in range(n * count // rest, (n + 1) * count // rest):
+                item(i)
+
+        zslot(PRE + n, False)
 
     @pl.when(jnp.logical_not(owner))
     def _():
@@ -166,8 +179,9 @@
         return remote(s2.at[j, way], r2.at[j, way], xsend.at[j, 1, way], xrecv.at[j, 1, way], (xright, xleft)[way])
 
     def product(j):
-        for way in range(2):
-            zarrived(j, 3, way)
+        for n in range(PIECES):
+            for way in range(2):
+                zarrived(j * PIECES + n, 3, way)
         a = jnp.concatenate([rows[j, b] for b in range(NZ)], axis=1)
 
         def times(dest):
@@ -179,13 +193,13 @@
         s1[j, 1] = far[HALF:]
         x1copy(j, 0).start()
         x1copy(j, 1).start()
-        slot = lax.rem(j, 4)
+        slot = lax.rem(j, 8)
         part[slot, 0] = times(xr)
         part[slot, 1] = times(xl)
         part[slot, 2] = times(x)
 
     def pass_on(j):
-        slot = lax.rem(j, 4)
+        slot = lax.rem(j, 8)
         x1copy(j, 0).wait_recv()
         s2[j, 0, :HALF] = (part[slot, 0, :HALF] + r1[j, 0].astype(jnp.float32)).astype(jnp.bfloat16)
         s2[j, 0, HALF:] = part[slot, 0, HALF:].astype(jnp.bfloat16)
@@ -196,25 +210,27 @@
         x2copy(j, 1).start()
 
     def finish(j):
-        slot = lax.rem(j, 4)
+        slot = lax.rem(j, 8)
         x2copy(j, 0).wait_recv()
         x2copy(j, 1).wait_recv()
         total = part[slot, 2] + r2[j, 0].astype(jnp.float32) + r2[j, 1].astype(jnp.float32)
         o_ref[pl.ds(pl.multiple_of(j * CH, CH), CH), :] = total
 
     def slot(t, carry):
-        zslot(t)
-        for lag, work in ((4, product), (5, pass_on), (6, finish)):
+        for n in range(PIECES):
+            zslot(t * PIECES + n)
+        for lag, work in ((FIRST, product), (FIRST + XLAG, pass_on), (FIRST + 2 * XLAG, finish)):
             j = t - lag
             pl.when(jnp.logical_and(j >= 0, j < NJ))(lambda j=j, work=work: work(j))
         return carry
 
-    lax.fori_loop(4, NJ + 6, slot, 0)
+    lax.fori_loop(FIRST, NJ + FIRST + 2 * XLAG, slot, 0)
 
     def drain(j, carry):
         for way in range(2):
-            for s in range(4):
-                zcopy(j, s, way).wait_send()
+            for n in range(PIECES):
+                for s in range(4):
+                    zcopy(j * PIECES + n, s, way).wait_send()
             x1copy(j, way).wait_send()
             x2copy(j, way).wait_send()
         return carry
@@ -239,18 +255,21 @@
     out = pl.pallas_call(
         kernel,
         out_shape=jax.ShapeDtypeStruct((2 * FEAT, SUB), f32),
-        in_specs=[pl.BlockSpec(memory_space=pltpu.VMEM)] * 2,
+        in_specs=[pl.BlockSpec(memory_space=pltpu.HBM)] * 2,
         out_specs=pl.BlockSpec(memory_space=pltpu.VMEM),
         scratch_shapes=[
+            pltpu.VMEM((TOK, FEAT), bf16),
+            pltpu.VMEM((TOK, FEAT), bf16),
+            dma((2,)),
             pltpu.VMEM((NJ, NZ, CH, TOK), bf16),
             pltpu.VMEM((NY, NZ, TOK, SUB), bf16),
-            pltpu.VMEM((4, 3, CH, SUB), f32),
+            pltpu.VMEM((8, 3, CH, SUB), f32),
             pltpu.VMEM((NJ, 2, HALF, SUB), bf16),
             pltpu.VMEM((NJ, 2, HALF, SUB), bf16),
             pltpu.VMEM((NJ, 2, CH, SUB), bf16),
             pltpu.VMEM((NJ, 2, CH, SUB), bf16),
-            dma((NJ, 4, 2)),
-            dma((NJ, 4, 2)),
+            dma((NJ * PIECES, 4, 2)),
+            dma((NJ * PIECES, 4, 2)),
             dma((NZ - 1,)),
             dma((NZ - 1,)),
             dma((NZ, 2, 2)),
@@ -267,7 +286,7 @@
             flops=2 * 2 * FEAT * 1024 * 1024, bytes_accessed=3 * 2**20, transcendentals=0
         ),
         name="stats",
-    )(quant_acts, full_acts)
+    )(*(pltpu.with_memory_space_constraint(a, pltpu.HBM) for a in (quant_acts, full_acts)))
     scale = 1.0 / (TOK * NX * NZ)
     return out[:FEAT] * scale, out[FEAT:] * scale
 

time: 97 us -> 79.4 us (0.82)
  Pallas kernels: 92.8 us -> 77.2 us
  local copies, waits for them, and re-layouts: 1.89 us -> 0 us
    pallas_call x1, Pallas kernels: 92.8 us -> 77.2 us  [local(): pl.pallas_call(kernel, out_shape=jax.ShapeDtypeStruct((2 * FEAT, SUB), f3...]
    unnamed x4 -> x0, local copies, waits for them, and re-layouts: 1.89 us -> none
where the time goes in v2:
time: 79.4 us; the launch traced here: 79.3 us
  Pallas kernels  77.2 us (97%)
  other arithmetic  1.45 us (2%)
    pallas_call x1, Pallas kernels, local(): pl.pallas_call(kernel, out_shape=jax.ShapeDtypeStruct((2 * FEAT, SUB), f3...  77.2 us

profile of v2, /device:TPU:2, one launch (start us, length us, event | category | flops | bytes accessed | tf_op | source)
XLA Modules:
  0.0 79.3 jit_solution(18395285229562635012)
XLA Ops:
  0.6 77.2 %stats.1 = f32[2048,256]{1,0:T(8,128)S(1)} custom-call(bf16[128,1024]{1,0:T(8,128)(2,1)} %q_hbm.1, bf16[128,1024]{1,0:T(8,128)(2,1)} %f_hbm.1), custom_call_target="tpu_custom_call" | custom-call | flops 4294967296 | bytes 3145728 | tf_op jit(solution)/shard_map/stats/pallas_call | solution.py:255
  77.8 1.5 %slice_multiply_fusion = (f32[1024,256]{1,0:T(8,128)}, f32[1024,256]{1,0:T(8,128)}) fusion(f32[2048,256]{1,0:T(8,128)S(1)} %stats.1), kind=kLoop, calls=%fused_computation | loop fusion | flops 524288 | bytes 4194304 | tf_op jit(solution)/shard_map/mul | solution.py:291

commit v3 on v2

--- a/solution.py
+++ b/solution.py
@@ -12,13 +12,13 @@
 NQ = FEAT // CH
 NJ = 2 * NQ
 HALF = CH // 2
-PIECES = 1
-ROWS = CH // PIECES
-LAG = 2
+AHEAD = (8, 6, 4, 2)
+EARLY, LATE = (0, 1, 2, 3), ()
 XLAG = 2
-YLAG = 3
-PRE = 0
-ORDER = (1, 7, 2, 6, 3, 5, 4)
+YLAG = 6
+WAVES = ((1, 7, 2, 6, 3, 5, 4),)
+WAVE_AT = (1,)
+ORDER = sum(WAVES, ())
 
 
 def wrap(v, n):
@@ -68,33 +68,30 @@
 
     pl.semaphore_wait(barrier, NZ - 1 + 5)
 
-    def zref(p, at, s, way):
-        j, start = lax.div(p, PIECES), lax.rem(p, PIECES) * ROWS
-        if s == 3:
-            return rows.at[j, at, pl.ds(pl.multiple_of(start + way * (ROWS // 2), ROWS // 2), ROWS // 2)]
-        return rows.at[j, at, pl.ds(pl.multiple_of(start, ROWS), ROWS)]
-
-    def zcopy(p, s, way):
-        ref = zref(p, wrap(z - s, NZ) if way == 0 else lax.rem(z + s, NZ), s, way)
-        return remote(ref, ref, zsend.at[p, s, way], zrecv.at[p, s, way], (right, left)[way])
-
-    def zarrived(p, s, way):
-        ref = zref(p, wrap(z - s - 1, NZ) if way == 0 else lax.rem(z + s + 1, NZ), s, way)
-        remote(ref, ref, zsend.at[p, s, way], zrecv.at[p, s, way], (right, left)[way]).wait_recv()
-
-    def zslot(t, guard=True):
-        for s in range(4):
-            p = t - s * LAG
-
-            def go(p=p, s=s):
+    def zref(j, at, s, way):
+        return rows.at[j, at, pl.ds(way * HALF, HALF)] if s == 3 else rows.at[j, at]
+
+    def zcopy(j, s, way):
+        ref = zref(j, wrap(z - s, NZ) if way == 0 else lax.rem(z + s, NZ), s, way)
+        return remote(ref, ref, zsend.at[j, s, way], zrecv.at[j, s, way], (right, left)[way])
+
+    def zarrived(j, s, way):
+        ref = zref(j, wrap(z - s - 1, NZ) if way == 0 else lax.rem(z + s + 1, NZ), s, way)
+        remote(ref, ref, zsend.at[j, s, way], zrecv.at[j, s, way], (right, left)[way]).wait_recv()
+
+    def zhops(t, steps):
+        for s in steps:
+            j = t + AHEAD[s]
+
+            def go(j=j, s=s):
                 for way in range(2):
                     if s > 0:
-                        zarrived(p, s - 1, way)
-                    zcopy(p, s, way).start()
-
-            if guard:
-                pl.when(jnp.logical_and(p >= 0, p < NJ * PIECES))(go)
-            elif p >= 0:
+                        zarrived(j, s - 1, way)
+                    zcopy(j, s, way).start()
+
+            if not isinstance(t, int):
+                pl.when(j < NJ)(go)
+            elif j >= 0:
                 go()
 
     def acopy(d):
@@ -102,15 +99,15 @@
         src = q_ref.at[:, pl.ds(pl.multiple_of(lax.rem(to, 4) * SUB, SUB), SUB)]
         return remote(src, cols.at[y, z], asend.at[d - 1], arecv.at[d - 1], dev(x, y, to, k))
 
-    for d in ORDER:
-        pl.when(lax.div(wrap(z + d, NZ), 4) == k)(lambda d=d: acopy(d).start())
+    def awave(n, what):
+        for d in WAVES[n]:
+            pl.when(lax.div(wrap(z + d, NZ), 4) == k)(lambda d=d: getattr(acopy(d), what)())
+
+    awave(0, "start")
 
     @pl.when(owner)
     def _():
         cols[y, z] = q_ref[:, pl.ds(pl.multiple_of(lax.rem(z, 4) * SUB, SUB), SUB)]
-
-    for t in range(PRE):
-        zslot(t, False)
 
     def ycopy(b, i, s, way):
         if s == 0:
@@ -155,15 +152,19 @@
                 yarrived(b, n, 1, way)
             kcopy(yo, b, n, 3).start()
 
-    FIRST = 4 * LAG // PIECES
-    count, rest = NZ + 2 * YLAG, FIRST * PIECES - PRE
-    for n in range(rest):
+    count, parts = NZ + 2 * YLAG, 2 * AHEAD[0]
+    for n in range(parts):
+        for wave in range(1, len(WAVES)):
+            if WAVE_AT[wave] == n:
+                awave(wave - 1, "wait_send")
+                awave(wave, "start")
+
         @pl.when(owner)
         def _():
-            for i in range(n * count // rest, (n + 1) * count // rest):
+            for i in range(n * count // parts, (n + 1) * count // parts):
                 item(i)
 
-        zslot(PRE + n, False)
+        zhops(n // 2 - AHEAD[0], (EARLY, LATE)[n % 2])
 
     @pl.when(jnp.logical_not(owner))
     def _():
@@ -179,9 +180,8 @@
         return remote(s2.at[j, way], r2.at[j, way], xsend.at[j, 1, way], xrecv.at[j, 1, way], (xright, xleft)[way])
 
     def product(j):
-        for n in range(PIECES):
-            for way in range(2):
-                zarrived(j * PIECES + n, 3, way)
+        for way in range(2):
+            zarrived(j, 3, way)
         a = jnp.concatenate([rows[j, b] for b in range(NZ)], axis=1)
 
         def times(dest):
@@ -217,27 +217,26 @@
         o_ref[pl.ds(pl.multiple_of(j * CH, CH), CH), :] = total
 
     def slot(t, carry):
-        for n in range(PIECES):
-            zslot(t * PIECES + n)
-        for lag, work in ((FIRST, product), (FIRST + XLAG, pass_on), (FIRST + 2 * XLAG, finish)):
+        zhops(t, EARLY)
+        pl.when(t < NJ)(lambda: product(t))
+        zhops(t, LATE)
+        for lag, work in ((XLAG, pass_on), (2 * XLAG, finish)):
             j = t - lag
             pl.when(jnp.logical_and(j >= 0, j < NJ))(lambda j=j, work=work: work(j))
         return carry
 
-    lax.fori_loop(FIRST, NJ + FIRST + 2 * XLAG, slot, 0)
+    lax.fori_loop(0, NJ + 2 * XLAG, slot, 0)
 
     def drain(j, carry):
         for way in range(2):
-            for n in range(PIECES):
-                for s in range(4):
-                    zcopy(j * PIECES + n, s, way).wait_send()
+            for s in range(4):
+                zcopy(j, s, way).wait_send()
             x1copy(j, way).wait_send()
             x2copy(j, way).wait_send()
         return carry
 
     lax.fori_loop(0, NJ, drain, 0)
-    for d in ORDER:
-        pl.when(lax.div(wrap(z + d, NZ), 4) == k)(lambda d=d: acopy(d).wait_send())
+    awave(len(WAVES) - 1, "wait_send")
 
     @pl.when(owner)
     def _():
@@ -268,8 +267,8 @@
             pltpu.VMEM((NJ, 2, HALF, SUB), bf16),
             pltpu.VMEM((NJ, 2, CH, SUB), bf16),
             pltpu.VMEM((NJ, 2, CH, SUB), bf16),
-            dma((NJ * PIECES, 4, 2)),
-            dma((NJ * PIECES, 4, 2)),
+            dma((NJ, 4, 2)),
+            dma((NJ, 4, 2)),
             dma((NZ - 1,)),
             dma((NZ - 1,)),
             dma((NZ, 2, 2)),

time: 79.4 us -> 79.1 us (level)
  Pallas kernels: 77.2 us -> 76.2 us
    pallas_call x1, Pallas kernels: 77.2 us -> 76.2 us  [local(): pl.pallas_call(kernel, out_shape=jax.ShapeDtypeStruct((2 * FEAT, SUB), f3...]
where the time goes in v3:
time: 79.1 us; the launch traced here: 78.3 us
  Pallas kernels  76.2 us (96%)
  other arithmetic  1.45 us (2%)
    pallas_call x1, Pallas kernels, local(): pl.pallas_call(kernel, out_shape=jax.ShapeDtypeStruct((2 * FEAT, SUB), f3...  76.2 us

profile of v3, /device:TPU:2, one launch (start us, length us, event | category | flops | bytes accessed | tf_op | source)
XLA Modules:
  0.0 78.3 jit_solution(2645519001720411822)
XLA Ops:
  0.6 76.2 %stats.1 = f32[2048,256]{1,0:T(8,128)S(1)} custom-call(bf16[128,1024]{1,0:T(8,128)(2,1)} %q_hbm.1, bf16[128,1024]{1,0:T(8,128)(2,1)} %f_hbm.1), custom_call_target="tpu_custom_call" | custom-call | flops 4294967296 | bytes 3145728 | tf_op jit(solution)/shard_map/stats/pallas_call | solution.py:254
  76.8 1.5 %slice_multiply_fusion = (f32[1024,256]{1,0:T(8,128)}, f32[1024,256]{1,0:T(8,128)}) fusion(f32[2048,256]{1,0:T(8,128)S(1)} %stats.1), kind=kLoop, calls=%fused_computation | loop fusion | flops 524288 | bytes 4194304 | tf_op jit(solution)/shard_map/mul | solution.py:290

commit v4 on v3

--- a/solution.py
+++ b/solution.py
@@ -58,13 +58,9 @@
     for to in (xright, xleft, up, down, other):
         pl.semaphore_signal(barrier, inc=1, device_id=to, device_id_type=MESH)
 
-    for copy in loads:
-        copy.wait()
+    loads[0].wait()
     for j in range(NQ):
-        qj = q_ref[:, j * CH : (j + 1) * CH].astype(jnp.float32)
-        fj = f_ref[:, j * CH : (j + 1) * CH].astype(jnp.float32)
-        rows[j, z] = qj.T.astype(jnp.bfloat16)
-        rows[NQ + j, z] = (fj - qj).astype(jnp.bfloat16).astype(jnp.float32).T.astype(jnp.bfloat16)
+        rows[j, z] = q_ref[:, j * CH : (j + 1) * CH].astype(jnp.float32).T.astype(jnp.bfloat16)
 
     pl.semaphore_wait(barrier, NZ - 1 + 5)
 
@@ -104,6 +100,11 @@
             pl.when(lax.div(wrap(z + d, NZ), 4) == k)(lambda d=d: getattr(acopy(d), what)())
 
     awave(0, "start")
+    loads[1].wait()
+    for j in range(NQ):
+        qj = q_ref[:, j * CH : (j + 1) * CH].astype(jnp.float32)
+        fj = f_ref[:, j * CH : (j + 1) * CH].astype(jnp.float32)
+        rows[NQ + j, z] = (fj - qj).astype(jnp.bfloat16).astype(jnp.float32).T.astype(jnp.bfloat16)
 
     @pl.when(owner)
     def _():

time: 79.1 us -> 79 us (level)
  no operation moved by 1% of the time
where the time goes in v4:
time: 79 us; the launch traced here: 78.3 us
  Pallas kernels  76.2 us (96%)
  other arithmetic  1.45 us (2%)
    pallas_call x1, Pallas kernels, local(): pl.pallas_call(kernel, out_shape=jax.ShapeDtypeStruct((2 * FEAT, SUB), f3...  76.2 us

profile of v4, /device:TPU:2, one launch (start us, length us, event | category | flops | bytes accessed | tf_op | source)
XLA Modules:
  0.0 78.3 jit_solution(662929906207220028)
XLA Ops:
  0.6 76.2 %stats.1 = f32[2048,256]{1,0:T(8,128)S(1)} custom-call(bf16[128,1024]{1,0:T(8,128)(2,1)} %q_hbm.1, bf16[128,1024]{1,0:T(8,128)(2,1)} %f_hbm.1), custom_call_target="tpu_custom_call" | custom-call | flops 4294967296 | bytes 3145728 | tf_op jit(solution)/shard_map/stats/pallas_call | solution.py:255
  76.9 1.5 %slice_multiply_fusion = (f32[1024,256]{1,0:T(8,128)}, f32[1024,256]{1,0:T(8,128)}) fusion(f32[2048,256]{1,0:T(8,128)S(1)} %stats.1), kind=kLoop, calls=%fused_computation | loop fusion | flops 524288 | bytes 4194304 | tf_op jit(solution)/shard_map/mul | solution.py:291
